TPU v7x, 32 devices: a whole 2x2x4 slice. The times are simulated.
32 devices in a mesh: parts: 2 (over x), lat: 16 (over z, y, core).
Axes of the slice: x: 2, y: 2, z: 4, core: 2. Of those that a mesh axis runs over, the one named last changes fastest.
Arguments:
- activations: bfloat16 [2, 1024, 1152], P(None, ('parts', 'lat')), parts along dimension 1, may hold values from -6 to 6
- enc_weight: bfloat16 [2, 1152, 65536], P(None, None, 'lat'), may hold values from -0.1875 to 0.1875
- enc_bias: float32 [2, 65536], P(None, 'lat'), may hold values from -1 to 0
- dec_weight: bfloat16 [3, 65536, 1152], P(None, 'lat'), may hold values from -0.0234375 to 0.0234375
- dec_bias: float32 [2, 1152], replicated, may hold values from -3 to 3
Outputs:
- reconstruction: float32 [1024, 2, 1152], P(('parts', 'lat')), parts along dimension 0
There are 2 independent parts, one for each index of `parts`. A program takes and returns all parts, laid end to end along the dimension named above; an argument that names none is the same for every part. Nothing has to cross between parts.
All inputs are finite; a program needn't handle non-finite values.
Results may differ from a plain program's by a relative error of at most 0.0022.
Values may be sent and summed in bfloat16 or wider, within the bound.
A program may use at most 128 MiB of HBM per device.

v0:
```python
import jax
import jax.numpy as jnp
from jax import lax
from jax.sharding import PartitionSpec as P


def pair_index(source_layer, target_layer):
    return target_layer * (target_layer + 1) // 2 + source_layer


def on_device(activations, enc_weight, enc_bias, dec_weight, dec_bias):
    layers = activations.shape[0]
    tok_rows = activations.shape[1]
    width = activations.shape[2]
    latent_codes = []
    for source_layer in range(layers):

        def encode(shard_rows, first_row, source_layer=source_layer):
            preact = jnp.dot(
                shard_rows, enc_weight[source_layer], preferred_element_type=jnp.float32
            )
            return jax.nn.relu(preact + enc_bias[source_layer]).astype(jnp.bfloat16)

        latent_codes.append(
            encode(
                lax.all_gather(activations[source_layer], "lat", axis=0, tiled=True), jnp.int32(0)
            )
        )

    def decode_target(target_layer, row_count):
        partial_sum = jnp.zeros((row_count, width), jnp.float32)
        for source_layer in range(target_layer + 1):
            code_rows = latent_codes[source_layer]
            partial_sum = partial_sum + jnp.dot(
                code_rows,
                dec_weight[pair_index(source_layer, target_layer)],
                preferred_element_type=jnp.float32,
            )
        return partial_sum

    targets_out = []
    for target_layer in range(layers):

        def decode(first_row, row_count, target_layer=target_layer):
            return decode_target(target_layer, row_count)

        summed = lax.psum_scatter(
            decode(jnp.int32(0), tok_rows * lax.axis_size("lat")),
            "lat",
            scatter_dimension=0,
            tiled=True,
        )
        targets_out.append(summed + dec_bias[target_layer])
    reconstruction = jnp.stack(targets_out, axis=1)
    return reconstruction


def solution(mesh):
    placed = (
        P(None, ("parts", "lat"), None),
        P(None, None, "lat"),
        P(None, "lat"),
        P(None, "lat", None),
        P(),
    )
    return jax.shard_map(
        on_device,
        mesh=mesh,
        in_specs=placed,
        out_specs=P(("parts", "lat"), None, None),
        check_vma=False,
    )
```

profile of v0, /device:TPU:0, one launch (start us, length us, event | category | flops | bytes accessed | tf_op | source)
XLA Modules:
  0.0 255.9 jit_solution(14380284684174763259)
XLA Ops:
  6.5 0.0 all-gather.5.cloned.1.call-start
  6.5 1.6 fusion.29
  8.1 0.0 all-gather.5.cloned.1.call-update
  8.1 0.0 all-gather.7.cloned.1.call-start
  8.2 0.7 all-gather.7.cloned.1.call-update
  8.9 0.0 reduce-scatter.5.cloned.1.call-start
  8.9 0.9 fusion.30
  9.8 40.9 %all-gather.5.cloned.1.call-done = bf16[1,512,1152]{2,1,0:T(8,128)(2,1)} async-done(((bf16[1,32,1152]{2,1,0:T(8,128)(2,1)}), bf16[1,512,1152]{2,1,0:T(8,128)(2,1)}) %all-gather.5.cloned.1.call-update) | async-done | bytes 1179664 | tf_op jit(solution)/shard_map/all_gather | solution.py:26
  50.7 9.9 %maximum_convert_fusion.1 = bf16[512,4096]{1,0:T(8,128)(2,1)} fusion(bf16[2,1152,4096]{2,1,0:T(8,128)(2,1)} %param.6, f32[4096]{0:T(1024)S(1)} %bitcast.40, bf16[1,512,1152]{2,1,0:T(8,128)(2,1)} %all-gather.5.cloned.1.call-done), kind=kOutput, calls=%fused_computation.16 | convolution fusion | flops 4838129664 | bytes 14827520 | tf_op jit(solution)/shard_map/dot_general | solution.py:19
  60.6 29.7 %all-gather.7.cloned.1.call-done = bf16[1,512,1152]{2,1,0:T(8,128)(2,1)} async-done(((bf16[1,32,1152]{2,1,0:T(8,128)(2,1)}), bf16[1,512,1152]{2,1,0:T(8,128)(2,1)}) %all-gather.7.cloned.1.call-update) | async-done | bytes 1179664 | tf_op jit(solution)/shard_map/all_gather | solution.py:26
  90.3 17.7 %fusion = f32[512,1152]{1,0:T(8,128)S(1)} fusion(bf16[3,4096,1152]{2,1,0:T(8,128)(2,1)} %param.8, bf16[2,1152,4096]{2,1,0:T(8,128)(2,1)} %param.6, f32[4096]{0:T(1024)S(1)} %bitcast.39, bf16[1,512,1152]{2,1,0:T(8,128)(2,1)} %all-gather.7.cloned.1.call-done), kind=kOutput, calls=%fused_computation | convolution fusion | flops 9669967872 | bytes 22429696 | tf_op jit(solution)/shard_map/dot_general | solution.py:34
  108.0 11.3 %fusion.19 = f32[512,1152]{1,0:T(8,128)} fusion(f32[512,1152]{1,0:T(8,128)S(1)} %fusion, bf16[512,4096]{1,0:T(8,128)(2,1)} %maximum_convert_fusion.1, bf16[3,4096,1152]{2,1,0:T(8,128)(2,1)} %param.8), kind=kOutput, calls=%fused_computation.17 | convolution fusion | flops 4832428032 | bytes 18350080 | tf_op jit(solution)/shard_map/dot_general | solution.py:34
  119.3 0.0 reduce-scatter.5.cloned.1.call-update
  119.3 0.0 copy-start
  119.4 0.0 reduce-scatter.3.cloned.1.call-start
  119.4 11.2 %fusion.6 = f32[512,1152]{1,0:T(8,128)} fusion(bf16[512,4096]{1,0:T(8,128)(2,1)} %maximum_convert_fusion.1, bf16[3,4096,1152]{2,1,0:T(8,128)(2,1)} %param.8), kind=kOutput, calls=%fused_computation.6 | convolution fusion | flops 4831838208 | bytes 15990784 | tf_op jit(solution)/shard_map/dot_general | solution.py:34
  130.6 0.0 reduce-scatter.3.cloned.1.call-update
  130.6 0.0 copy-done
  130.7 50.7 %reduce-scatter.5.cloned.1.call-done = f32[32,1152]{1,0:T(8,128)} async-done(((f32[512,1152]{1,0:T(8,128)}), f32[32,1152]{1,0:T(8,128)}) %reduce-scatter.5.cloned.1.call-update) | async-done | bytes 147472 | tf_op jit(solution)/shard_map/reduce_scatter | solution.py:47
  181.4 0.9 add_bitcast_fusion
  182.3 65.2 %reduce-scatter.3.cloned.1.call-done = f32[32,1152]{1,0:T(8,128)} async-done(((f32[512,1152]{1,0:T(8,128)}), f32[32,1152]{1,0:T(8,128)}) %reduce-scatter.3.cloned.1.call-update) | async-done | bytes 147472 | tf_op jit(solution)/shard_map/reduce_scatter | solution.py:47
  247.5 0.9 add_bitcast_fusion.1
  248.4 0.9 copy.6
  (2 shorter events, 0.1 us)
Async XLA Ops:
  6.5 44.2 %all-gather.5.cloned.1.call-start = ((), (), s32[]{:S(2)}) async-start(), calls=%async_computation.4 | async-start | bytes 1253376 | tf_op jit(solution)/shard_map/all_gather | solution.py:26
  8.1 82.1 %all-gather.7.cloned.1.call-start = ((), (), s32[]{:S(2)}) async-start(), calls=%async_computation.5 | async-start | bytes 1253376 | tf_op jit(solution)/shard_map/all_gather | solution.py:26
  8.9 172.5 %reduce-scatter.5.cloned.1.call-start = ((), (), s32[]{:S(2)}) async-start(), calls=%async_computation.3 | async-start | bytes 2506752 | tf_op jit(solution)/shard_map/reduce_scatter | solution.py:47
  119.3 11.3 %copy-start = (f32[2,1152]{1,0:T(2,128)S(1)}, f32[2,1152]{1,0:T(2,128)}, u32[]{:S(2)}) copy-start(f32[2,1152]{1,0:T(2,128)} %param.9) | copy-start | bytes 27652
  119.4 128.1 %reduce-scatter.3.cloned.1.call-start = ((), (), s32[]{:S(2)}) async-start(), calls=%async_computation.2 | async-start | bytes 2506752 | tf_op jit(solution)/shard_map/reduce_scatter | solution.py:47
Sparse Core Ops, SparseCore 0:
  9.6 41.0 all-gather.4
  53.0 37.2 all-gather.6
  119.5 61.8 reduce-scatter.4
  185.5 61.9 reduce-scatter.2
where the time goes:
time: 256 us
  waiting for transfers between devices  187 us (73%)
  matrix products  50.1 us (20%)
  between operations  13.2 us (5%)
  local copies, waits for them, and re-layouts  3.42 us (1%)
    reduce_scatter x2, waiting for transfers between devices, on_device(): lax.psum_scatter(decode(jnp.int32(0), tok_rows * lax.axis_size('lat')), '...  116 us
    all_gather x2, waiting for transfers between devices, on_device(): lax.all_gather(activations[source_layer], 'lat', axis=0, tiled=True)  70.6 us
    dot_general x3, matrix products, decode_target(): jnp.dot(code_rows, dec_weight[pair_index(source_layer, target_layer)], pr...  40.2 us
    dot_general x1, matrix products, encode(): jnp.dot(shard_rows, enc_weight[source_layer], preferred_element_type=jnp....  9.89 us
  transfers between devices with their start and end apart: 4, of which 4 were waited for; matrix products, arithmetic and copies ran while one was open for 9% of the time, Pallas kernels for 0%

commit v1 on v0

v1 whole, which is shorter than its diff:
```python
import functools

import jax
import jax.numpy as jnp
from jax import lax
from jax.experimental import pallas as pl
from jax.experimental.pallas import tpu as pltpu
from jax.sharding import PartitionSpec as P

ENC_COLS = 512
OUT_COLS = 256
DEPTH = 2048


def pair_index(source_layer, target_layer):
    return target_layer * (target_layer + 1) // 2 + source_layer


def kernel(
    n, pieces,
    act, enc_w, enc_b, dec_w, dec_b,
    out,
    x, enc_buf, dec_buf, codes, part, core_in, y_out, y_in, z_out, z_in,
    own_sem, enc_sem, dec_sem,
    gz_s, gz_r, gy_s, gy_r, gc_s, gc_r,
    rc_s, rc_r, ry_s, ry_r, rz_s, rz_r,
):
    layers, rows, width = act.shape
    depth = n // 4
    chunks = enc_buf.shape[0]
    me = lax.axis_index("lat")
    c = lax.rem(me, 2)
    y = lax.rem(lax.div(me, 2), 2)
    z = lax.div(me, 4)

    def rank(zz, yy, cc):
        return zz * 4 + yy * 2 + cc

    def z_at(step):
        return lax.rem(z + step + depth, depth)

    y_peer = rank(z, 1 - y, c)
    c_peer = rank(z, y, 1 - c)
    z_peers = [rank(z_at(d), y, c) for d in range(depth)]
    z_froms = [rank(z_at(-d), y, c) for d in range(depth)]
    y_froms = [rank(z_at(-d), 1 - y, c) for d in range(depth)]

    def rows_of(l, r):
        return x.at[l, pl.ds(pl.multiple_of(r * rows, rows), rows)]

    def remote(src, dst, s, r, dev):
        return pltpu.make_async_remote_copy(
            src_ref=src, dst_ref=dst, send_sem=s, recv_sem=r,
            device_id={"lat": dev}, device_id_type=pl.DeviceIdType.MESH,
        )

    sent = []

    def start(copy):
        copy.start()
        sent.append(copy)

    def enc_copy(l, j):
        return pltpu.make_async_copy(
            enc_w.at[l, :, pl.ds(pl.multiple_of(j * ENC_COLS, ENC_COLS), ENC_COLS)],
            enc_buf.at[j], enc_sem.at[l, j],
        )

    def dec_copy(p):
        return pltpu.make_async_copy(dec_w.at[p], dec_buf.at[p], dec_sem.at[p])

    barrier = pltpu.get_barrier_semaphore()
    for dev in z_peers[1:] + [y_peer, c_peer]:
        pl.semaphore_signal(
            barrier, inc=1, device_id={"lat": dev}, device_id_type=pl.DeviceIdType.MESH
        )
    own = [pltpu.make_async_copy(act.at[l], rows_of(l, me), own_sem.at[l]) for l in range(layers)]
    for copy in own:
        copy.start()
    for j in range(chunks):
        enc_copy(0, j).start()
    pl.semaphore_wait(barrier, depth + 1)

    def gather_z(l):
        for d in range(1, depth):
            start(remote(act.at[l], rows_of(l, me), gz_s.at[l, d], gz_r.at[l, d], z_peers[d]))
        start(remote(act.at[l], rows_of(l, me), gy_s.at[l, 0], gy_r.at[l, 0], y_peer))
        start(remote(act.at[l], rows_of(l, me), gc_s.at[l, 0], gc_r.at[l, 0], c_peer))

    def gather_y(l):
        for d in range(1, depth):
            block = rows_of(l, z_froms[d])
            remote(block, block, gz_s.at[l, d], gz_r.at[l, d], me).wait_recv()
            start(remote(block, block, gy_s.at[l, d], gy_r.at[l, d], y_peer))
            start(remote(block, block, gc_s.at[l, d], gc_r.at[l, d], c_peer))

    def gather_core(l):
        for d in range(depth):
            block = rows_of(l, y_froms[d])
            remote(block, block, gy_s.at[l, d], gy_r.at[l, d], me).wait_recv()
            start(remote(block, block, gc_s.at[l, depth + d], gc_r.at[l, depth + d], c_peer))

    def gather_end(l):
        own[l].wait()
        for d in range(2 * depth):
            yy = y if d < depth else 1 - y
            block = rows_of(l, rank(z_at(-(d % depth)), yy, 1 - c))
            remote(block, block, gc_s.at[l, d], gc_r.at[l, d], me).wait_recv()

    def encode(l, first, last):
        def body(j, carry):
            enc_copy(l, j).wait()
            cols = pl.ds(pl.multiple_of(j * ENC_COLS, ENC_COLS), ENC_COLS)
            pre = jnp.dot(x[l], enc_buf[j], preferred_element_type=jnp.float32)
            code = jnp.maximum(pre + enc_b[l : l + 1, cols], 0.0)
            codes[l, :, cols] = code.astype(jnp.bfloat16)
            if l + 1 < layers:
                enc_copy(l + 1, j).start()
            return carry

        lax.fori_loop(first, last, body, 0)

    def decode(q, s):
        t, at, wide = pieces[q]
        p = pair_index(s, t)
        step = min(DEPTH, codes.shape[2])
        total = None
        for k in range(0, codes.shape[2], step):
            term = jnp.dot(
                codes[s, :, k : k + step],
                dec_buf[p, k : k + step, at : at + wide],
                preferred_element_type=jnp.float32,
            )
            total = term if total is None else total + term
        total = total.reshape(depth, 2, 2, rows, wide)
        if s > 0:
            total = total + part[q, :, :, :, :, :wide]
        part[q, :, :, :, :, :wide] = total

    def to_core(q):
        wide = pieces[q][2]
        return remote(
            part.at[q, :, :, 1 - c, :, pl.ds(0, wide)], core_in.at[q, :, :, :, pl.ds(0, wide)],
            rc_s.at[q], rc_r.at[q], c_peer,
        )

    def to_y(q):
        cols = pl.ds(0, pieces[q][2])
        return remote(
            y_out.at[q, :, :, cols], y_in.at[q, :, :, cols], ry_s.at[q], ry_r.at[q], y_peer
        )

    def to_z(q, d):
        cols = pl.ds(0, pieces[q][2])
        return remote(
            z_out.at[q, z_at(d), :, cols], z_in.at[q, d, :, cols],
            rz_s.at[q, d], rz_r.at[q, d], z_peers[d],
        )

    def stage_core(q):
        start(to_core(q))

    def stage_y(q):
        wide = pieces[q][2]
        to_core(q).wait_recv()
        away = part[q, :, 1 - y, c, :, :wide] + core_in[q, :, 1 - y, :, :wide]
        y_out[q, :, :, :wide] = away.astype(jnp.bfloat16)
        start(to_y(q))
        part[q, :, y, c, :, :wide] = part[q, :, y, c, :, :wide] + core_in[q, :, y, :, :wide]

    def stage_z(q):
        wide = pieces[q][2]
        to_y(q).wait_recv()
        total = part[q, :, y, c, :, :wide] + y_in[q, :, :, :wide].astype(jnp.float32)
        z_out[q, :, :, :wide] = total.astype(jnp.bfloat16)
        for d in range(1, depth):
            start(to_z(q, d))
        part[q, :, y, c, :, :wide] = total

    def stage_out(q):
        t, at, wide = pieces[q]
        total = part[q, z, y, c, :, :wide] + dec_b[t : t + 1, at : at + wide]
        for d in range(1, depth):
            to_z(q, d).wait_recv()
            total = total + z_in[q, d, :, :wide].astype(jnp.float32)
        out[t, :, at : at + wide] = total

    stages = (stage_core, stage_y, stage_z, stage_out)
    offsets = (0, 1, 3, 5)
    due = []
    clock = [0]

    def tick():
        now = [e for e in due if e[0] <= clock[0]]
        for e in sorted(now):
            due.remove(e)
            stages[e[2]](e[1])
        clock[0] += 1

    def finished(q):
        for k, o in enumerate(offsets):
            due.append((clock[0] + o, q, k))

    gather_z(0)
    gather_y(0)
    gather_core(0)
    dec_copy(0).start()
    for l in range(1, layers):
        gather_z(l)
    gather_end(0)

    half = chunks // 2
    for t in range(layers):
        if t == 0:
            encode(0, 0, half)
            for l in range(1, layers):
                gather_y(l)
            encode(0, half, chunks)
            for p in range(1, dec_buf.shape[0]):
                dec_copy(p).start()
        else:
            if t == 1:
                for l in range(1, layers):
                    gather_core(l)
            gather_end(t)
            for a in range(0, chunks, 2):
                encode(t, a, a + 2)
                tick()
        for s in range(t + 1):
            dec_copy(pair_index(s, t)).wait()
        for q in range(len(pieces)):
            if pieces[q][0] != t:
                continue
            for s in range(t + 1):
                decode(q, s)
                if s == t:
                    finished(q)
                tick()
    while due:
        tick()
    for copy in sent:
        copy.wait_send()


def on_device(activations, enc_weight, enc_bias, dec_weight, dec_bias):
    layers, rows, width = activations.shape
    latents = enc_weight.shape[2]
    pairs = dec_weight.shape[0]
    n = lax.axis_size("lat")
    depth = n // 4
    tokens = n * rows
    chunks = latents // ENC_COLS
    pieces = [
        (t, at, min(OUT_COLS, width - at)) for t in range(layers) for at in range(0, width, OUT_COLS)
    ]
    count = len(pieces)
    vmem = pl.BlockSpec(memory_space=pltpu.VMEM)
    hbm = pl.BlockSpec(memory_space=pl.ANY)
    dma = pltpu.SemaphoreType.DMA
    bf16, f32 = jnp.bfloat16, jnp.float32
    result = pl.pallas_call(
        functools.partial(kernel, n, pieces),
        out_shape=jax.ShapeDtypeStruct((layers, rows, width), f32),
        in_specs=[hbm, hbm, vmem, hbm, vmem],
        out_specs=vmem,
        scratch_shapes=[
            pltpu.VMEM((layers, tokens, width), bf16),
            pltpu.VMEM((chunks, width, ENC_COLS), bf16),
            pltpu.VMEM((pairs, latents, width), bf16),
            pltpu.VMEM((layers, tokens, latents), bf16),
            pltpu.VMEM((count, depth, 2, 2, rows, OUT_COLS), f32),
            pltpu.VMEM((count, depth, 2, rows, OUT_COLS), f32),
            pltpu.VMEM((count, depth, rows, OUT_COLS), bf16),
            pltpu.VMEM((count, depth, rows, OUT_COLS), bf16),
            pltpu.VMEM((count, depth, rows, OUT_COLS), bf16),
            pltpu.VMEM((count, depth, rows, OUT_COLS), bf16),
            dma((layers,)),
            dma((layers, chunks)),
            dma((pairs,)),
            dma((layers, depth)), dma((layers, depth)),
            dma((layers, depth)), dma((layers, depth)),
            dma((layers, 2 * depth)), dma((layers, 2 * depth)),
            dma((count,)), dma((count,)),
            dma((count,)), dma((count,)),
            dma((count, depth)), dma((count, depth)),
        ],
        compiler_params=pltpu.CompilerParams(
            collective_id=0, has_side_effects=True, vmem_limit_bytes=63 * 1024 * 1024
        ),
        cost_estimate=pl.CostEstimate(
            flops=2 * tokens * latents * width * (layers + pairs),
            bytes_accessed=2 * latents * width * (layers + pairs),
            transcendentals=0,
        ),
    )(activations, enc_weight, enc_bias, dec_weight, dec_bias)
    return jnp.transpose(result, (1, 0, 2))


def solution(mesh):
    placed = (
        P(None, ("parts", "lat"), None),
        P(None, None, "lat"),
        P(None, "lat"),
        P(None, "lat", None),
        P(),
    )
    return jax.shard_map(
        on_device,
        mesh=mesh,
        in_specs=placed,
        out_specs=P(("parts", "lat"), None, None),
        check_vma=False,
    )
```

time: 256 us -> 83.5 us (0.33)
  waiting for transfers between devices: 187 us -> 0 us
  Pallas kernels: 0 us -> 81.4 us
  matrix products: 50.1 us -> 0 us
  between operations: 13.2 us -> 0.01 us
    reduce_scatter x2 -> x0, waiting for transfers between devices: 116 us -> none  [on_device(): lax.psum_scatter(decode(jnp.int32(0), tok_rows * lax.axis_size('lat')), '...]
    pallas_call x0 -> x1, Pallas kernels: none -> 81.4 us  [on_device(): pl.pallas_call(functools.partial(kernel, n, pieces), out_shape=jax.ShapeD...]
    all_gather x2 -> x0, waiting for transfers between devices: 70.6 us -> none  [on_device(): lax.all_gather(activations[source_layer], 'lat', axis=0, tiled=True)]
    dot_general x4 -> x0, matrix products: 50.1 us -> none  [the longest x3 40.2 us: decode_target(): jnp.dot(code_rows, dec_weight[pair_index(source_layer, target_layer)], pr...]
  transfers between devices with their start and end apart: 4 -> 0, of which waited for: 4 -> 0; matrix products, arithmetic and copies ran while one was open for 9% -> 0% of each run, Pallas kernels for 0% -> 0%
where the time goes in v1:
time: 83.5 us; the launch traced here: 83.3 us
  Pallas kernels  81.4 us (97%)
  local copies, waits for them, and re-layouts  1.9 us (2%)
    pallas_call x1, Pallas kernels, on_device(): pl.pallas_call(functools.partial(kernel, n, pieces), out_shape=jax.ShapeD...  81.4 us
    transpose x1, local copies, waits for them, and re-layouts, on_device(): return jnp.transpose(result, (1, 0, 2))  1.9 us

profile of v1, /device:TPU:0, one launch (start us, length us, event | category | flops | bytes accessed | tf_op | source)
XLA Modules:
  0.0 83.3 jit_solution(11717605145774774201)
XLA Ops:
  0.0 81.4 %shard_map.55 = f32[2,32,1152]{2,1,0:T(8,128)} custom-call(bf16[2,32,1152]{2,1,0:T(8,128)(2,1)} %act.1, bf16[2,1152,4096]{2,1,0:T(8,128)(2,1)} %enc_w.1, f32[2,4096]{1,0:T(2,128)} %enc_b.1, bf16[3,4096,1152]{2,1,0:T(8,128)(2,1)} %dec_w.1, f32[2,1152]{1,0:T(2,128)} %dec_b.1), custom_call_target="tpu_custom_call" | custom-call | flops 24159191040 | bytes 47185920 | tf_op jit(solution)/shard_map/pallas_call | solution.py:261
  81.4 1.9 %copy.6 = f32[32,2,1152]{2,1,0:T(2,128)} copy(f32[32,2,1152]{2,0,1:T(8,128)} %bitcast.1) | data formatting | bytes 589824 | tf_op jit(solution)/shard_map/transpose | solution.py:296

commit v2 on v1

--- a/solution.py
+++ b/solution.py
@@ -186,7 +186,7 @@
         out[t, :, at : at + wide] = total
 
     stages = (stage_core, stage_y, stage_z, stage_out)
-    offsets = (0, 1, 3, 5)
+    offsets = (0, 2, 6, 10)
     due = []
     clock = [0]
 

time: 83.5 us -> 82.1 us (0.983)
  Pallas kernels: 81.4 us -> 80 us
    pallas_call x1, Pallas kernels: 81.4 us -> 80 us  [on_device(): pl.pallas_call(functools.partial(kernel, n, pieces), out_shape=jax.ShapeD...]
where the time goes in v2:
time: 82.1 us; the launch traced here: 81.9 us
  Pallas kernels  80 us (97%)
  local copies, waits for them, and re-layouts  1.9 us (2%)
    pallas_call x1, Pallas kernels, on_device(): pl.pallas_call(functools.partial(kernel, n, pieces), out_shape=jax.ShapeD...  80 us
    transpose x1, local copies, waits for them, and re-layouts, on_device(): return jnp.transpose(result, (1, 0, 2))  1.9 us

profile of v2, /device:TPU:0, one launch (start us, length us, event | category | flops | bytes accessed | tf_op | source)
XLA Modules:
  0.0 81.9 jit_solution(7290019855539970087)
XLA Ops:
  0.0 80.0 %shard_map.55 = f32[2,32,1152]{2,1,0:T(8,128)} custom-call(bf16[2,32,1152]{2,1,0:T(8,128)(2,1)} %act.1, bf16[2,1152,4096]{2,1,0:T(8,128)(2,1)} %enc_w.1, f32[2,4096]{1,0:T(2,128)} %enc_b.1, bf16[3,4096,1152]{2,1,0:T(8,128)(2,1)} %dec_w.1, f32[2,1152]{1,0:T(2,128)} %dec_b.1), custom_call_target="tpu_custom_call" | custom-call | flops 24159191040 | bytes 47185920 | tf_op jit(solution)/shard_map/pallas_call | solution.py:261
  80.0 1.9 %copy.6 = f32[32,2,1152]{2,1,0:T(2,128)} copy(f32[32,2,1152]{2,0,1:T(8,128)} %bitcast.1) | data formatting | bytes 589824 | tf_op jit(solution)/shard_map/transpose | solution.py:296
